TPU v7x, 256 devices: a whole 4x4x8 slice. The times are simulated.
256 devices in a mesh: seq: 64 (over y_lo, x, z), dp: 4 (over y_hi, core).
Axes of the slice: x: 4, y: 4 (y_hi: 2, y_lo: 2; y = y_hi * 2 + y_lo), z: 8, core: 2. Of those that a mesh axis runs over, the one named last changes fastest.
Arguments:
- signal: float32 [4, 65536, 384], P('dp', 'seq'), may hold values from -6 to 6
- gate_values: float32 [4, 65536, 384], P('dp', 'seq'), may hold values from -6 to 6
- cotangent: float32 [4, 65536, 384], P('dp', 'seq'), may hold values from -6 to 6
- kernel: float32 [128, 512, 384], P(None, 'seq'), may hold values from -6 to 6
- first_factor: float32 [128, 128], replicated, may hold values from -0.5 to 0.5
- second_factor: float32 [512, 512], replicated, may hold values from -0.25 to 0.25
Outputs:
- grad_signal: float32 [4, 65536, 384], P('dp', 'seq')
- grad_gates: float32 [4, 65536, 384], P('dp', 'seq')
- grad_kernel: float32 [128, 512, 384], P('dp', 'seq')
- grad_first: float32 [128, 128], replicated
- grad_second: float32 [512, 512], replicated
All inputs are finite; a program needn't handle non-finite values.
Results may differ from a plain program's by a relative error of at most 0.000071.
Values sent between devices are 32-bit elements; how exact they have to be, the bound alone decides.
No kernel may reach another device: no remote copies, remote signals or barrier semaphores. Data moves between devices by JAX's collectives and lax.ppermute only.
A program may use at most 128 MiB of HBM per device.

v0:
```python
import math
import jax
import jax.numpy as jnp
from jax import lax
from jax.sharding import PartitionSpec as P


def along_second(data, factor):
    return jnp.einsum("bijc,kj->bikc", data, factor, precision=lax.Precision.HIGHEST)


def along_second_t(data, factor):
    return jnp.einsum("bikc,kj->bijc", data, factor, precision=lax.Precision.HIGHEST)


def along_first(factor, data):
    return jnp.einsum("mi,bikc->bmkc", factor, data, precision=lax.Precision.HIGHEST)


def along_first_t(factor, data):
    return jnp.einsum("mi,bmkc->bikc", factor, data, precision=lax.Precision.HIGHEST)


def outer_first(left, right):
    return jnp.einsum("bmkc,bikc->mi", left, right, precision=lax.Precision.HIGHEST)


def outer_second(left, right):
    return jnp.einsum("bikc,bijc->kj", left, right, precision=lax.Precision.HIGHEST)


def body(signal, gate_values, cotangent, kernel, first_factor, second_factor):
    batch = signal.shape[0]
    blocks = first_factor.shape[0]
    block = second_factor.shape[0]
    channels = signal.shape[2]
    local_rows = signal.shape[1] // block
    shape_rows = (batch, local_rows, block, channels)
    source = signal.reshape(shape_rows)
    gating = gate_values.reshape(shape_rows)
    upstream = cotangent.reshape(shape_rows)
    whole = lax.all_to_all(source, "seq", split_axis=3, concat_axis=1, tiled=True)
    kernel_cols = lax.all_to_all(kernel, "seq", split_axis=2, concat_axis=1, tiled=True)
    section_one = along_second(whole, second_factor)
    spectrum = along_first(first_factor, section_one)
    weighted = kernel_cols[None] * spectrum
    back_one = along_first_t(first_factor, weighted)
    full_mixed = along_second_t(back_one, second_factor)
    mixed = lax.all_to_all(full_mixed, "seq", split_axis=1, concat_axis=3, tiled=True)
    grad_mixed = upstream * gating
    grad_gate = upstream * mixed
    grad_whole = lax.all_to_all(grad_mixed, "seq", split_axis=3, concat_axis=1, tiled=True)
    grad_back = along_second(grad_whole, second_factor)
    second_grad = outer_second(back_one, grad_whole)
    grad_weighted = along_first(first_factor, grad_back)
    first_grad = outer_first(weighted, grad_back)
    kernel_cols_grad = jnp.sum(grad_weighted * spectrum, axis=0)
    grad_spectrum = grad_weighted * kernel_cols[None]
    grad_section = along_first_t(first_factor, grad_spectrum)
    first_grad = first_grad + outer_first(grad_spectrum, section_one)
    grad_full = along_second_t(grad_section, second_factor)
    second_grad = second_grad + outer_second(grad_section, whole)
    grad_source = lax.all_to_all(grad_full, "seq", split_axis=1, concat_axis=3, tiled=True)
    kernel_term = lax.all_to_all(kernel_cols_grad, "seq", split_axis=1, concat_axis=2, tiled=True)
    grad_kernel = lax.psum_scatter(kernel_term, "dp", scatter_dimension=0, tiled=True)
    first_total, second_total = lax.psum((first_grad, second_grad), ("seq", "dp"))
    sequences = batch * lax.axis_size("dp")
    first_scale = 1.0 / math.sqrt(sequences * block * channels)
    second_scale = 1.0 / math.sqrt(sequences * blocks * channels)
    return (
        grad_source.reshape(signal.shape),
        grad_gate.reshape(signal.shape),
        grad_kernel,
        first_total * first_scale,
        second_total * second_scale,
    )


def solution(mesh):
    in_specs = (
        P("dp", "seq", None),
        P("dp", "seq", None),
        P("dp", "seq", None),
        P(None, "seq", None),
        P(),
        P(),
    )
    out_specs = (P("dp", "seq", None), P("dp", "seq", None), P("dp", "seq", None), P(), P())
    return jax.shard_map(body, mesh=mesh, in_specs=in_specs, out_specs=out_specs, check_vma=False)
```

profile of v0, /device:TPU:6, one launch (start us, length us, event | category | flops | bytes accessed | tf_op | source)
XLA Modules:
  0.0 535.5 jit_solution(2666855981043520354)
XLA Ops:
  8.0 3.8 copy.114
  11.8 13.0 %all-to-all-start.3 = ((f32[1,2,512,384]{2,1,0,3:T(2,128)}), f32[1,2,512,384]{2,1,0,3:T(2,128)S(1)}, u32[]{:S(2)}, u32[]{:S(2)}) async-start(f32[1,2,512,384]{2,1,0,3:T(2,128)} %copy.114), calls=%async_computation.3 | async-start | bytes 3145728 | tf_op jit(solution)/shard_map/all_to_all | solution.py:42
  24.8 3.2 mul.41
  28.0 3.7 copy.113
  31.7 32.9 %all-to-all-done.3 = f32[1,2,512,384]{2,1,0,3:T(2,128)S(1)} async-done(((f32[1,2,512,384]{2,1,0,3:T(2,128)}), f32[1,2,512,384]{2,1,0,3:T(2,128)S(1)}, u32[]{:S(2)}, u32[]{:S(2)}) %all-to-all-start.3) | async-done | bytes 1572896 | tf_op jit(solution)/shard_map/all_to_all | solution.py:42
  64.6 6.6 %all-to-all-start = ((f32[1,2,512,384]{2,1,0,3:T(2,128)}), f32[1,2,512,384]{2,1,0,3:T(2,128)}, u32[]{:S(2)}, u32[]{:S(2)}) async-start(f32[1,2,512,384]{2,1,0,3:T(2,128)} %copy.113), calls=%async_computation | async-start | bytes 3145728 | tf_op jit(solution)/shard_map/all_to_all | solution.py:52
  74.3 35.7 %all-to-all-done = f32[1,2,512,384]{2,1,0,3:T(2,128)} async-done(((f32[1,2,512,384]{2,1,0,3:T(2,128)}), f32[1,2,512,384]{2,1,0,3:T(2,128)}, u32[]{:S(2)}, u32[]{:S(2)}) %all-to-all-start) | async-done | bytes 1572896 | tf_op jit(solution)/shard_map/all_to_all | solution.py:52
  110.0 6.3 %all-to-all-start.1 = ((f32[128,8,384]{0,1,2:T(8,128)}), f32[128,8,384]{0,1,2:T(8,128)S(1)}, u32[]{:S(2)}, u32[]{:S(2)}) async-start(f32[128,8,384]{0,1,2:T(8,128)} %copy.87), calls=%async_computation.1 | async-start | bytes 3145728 | tf_op jit(solution)/shard_map/all_to_all | solution.py:43
  119.4 3.1 reshape.99
  125.6 3.3 reshape.93
  129.0 4.2 fusion.44
  143.9 10.8 %all-to-all-done.1 = f32[128,8,384]{0,1,2:T(8,128)S(1)} async-done(((f32[128,8,384]{0,1,2:T(8,128)}), f32[128,8,384]{0,1,2:T(8,128)S(1)}, u32[]{:S(2)}, u32[]{:S(2)}) %all-to-all-start.1) | async-done | bytes 1572896 | tf_op jit(solution)/shard_map/all_to_all | solution.py:43
  154.6 6.9 %all-to-all-start.5 = ((f32[128,512,6]{0,2,1:T(8,128)}), f32[128,512,6]{0,2,1:T(8,128)}, u32[]{:S(2)}, u32[]{:S(2)}) async-start(f32[128,512,6]{0,2,1:T(8,128)} %copy.98), calls=%async_computation.5 | async-start | bytes 4194304 | tf_op jit(solution)/shard_map/all_to_all | solution.py:64
  171.1 38.3 %all-to-all-done.5 = f32[128,512,6]{0,2,1:T(8,128)} async-done(((f32[128,512,6]{0,2,1:T(8,128)}), f32[128,512,6]{0,2,1:T(8,128)}, u32[]{:S(2)}, u32[]{:S(2)}) %all-to-all-start.5) | async-done | bytes 1572896 | tf_op jit(solution)/shard_map/all_to_all | solution.py:64
  209.4 6.8 %all-to-all-start.4 = ((f32[1,128,512,6]{2,0,3,1:T(1,128)}), f32[1,128,512,6]{2,0,3,1:T(1,128)}, u32[]{:S(2)}, u32[]{:S(2)}) async-start(f32[1,128,512,6]{2,0,3,1:T(1,128)} %copy.95), calls=%async_computation.4 | async-start | bytes 3145728 | tf_op jit(solution)/shard_map/all_to_all | solution.py:49
  216.6 4.7 fusion.25
  225.6 3.4 fusion.40
  229.0 3.7 fusion.31
  243.5 9.3 %all-to-all-done.4 = f32[1,128,512,6]{2,0,3,1:T(1,128)} async-done(((f32[1,128,512,6]{2,0,3,1:T(1,128)}), f32[1,128,512,6]{2,0,3,1:T(1,128)}, u32[]{:S(2)}, u32[]{:S(2)}) %all-to-all-start.4) | async-done | bytes 1572896 | tf_op jit(solution)/shard_map/all_to_all | solution.py:49
  252.7 6.8 %all-to-all-start.2 = ((f32[1,128,512,6]{2,0,3,1:T(1,128)}), f32[1,128,512,6]{2,0,3,1:T(1,128)S(1)}, u32[]{:S(2)}, u32[]{:S(2)}) async-start(f32[1,128,512,6]{2,0,3,1:T(1,128)} %copy.90), calls=%async_computation.2 | async-start | bytes 3145728 | tf_op jit(solution)/shard_map/all_to_all | solution.py:63
  262.6 242.0 %all-reduce.3.cloned.1.call-done = (f32[128,128]{1,0:T(8,128)}, f32[512,512]{1,0:T(8,128)}) async-done(((f32[128,128]{1,0:T(8,128)}, f32[512,512]{1,0:T(8,128)}), (f32[128,128]{1,0:T(8,128)}, f32[512,512]{1,0:T(8,128)})) %all-reduce.3.cloned.1.call-update) | async-done | bytes 1114128 | tf_op jit(solution)/shard_map/psum | solution.py:66
  508.4 3.4 copy.124
  511.8 3.4 all_to_all.85
  515.2 3.4 mul.45
  (62 shorter events, 60.9 us)
Async XLA Ops:
  8.0 120.9 %copy-start = (f32[512,512]{1,0:T(8,128)S(1)}, f32[512,512]{1,0:T(8,128)}, u32[]{:S(2)}) copy-start(f32[512,512]{1,0:T(8,128)} %param.11) | copy-start | bytes 3145732
  11.8 52.8 %all-to-all-start.3 = ((f32[1,2,512,384]{2,1,0,3:T(2,128)}), f32[1,2,512,384]{2,1,0,3:T(2,128)S(1)}, u32[]{:S(2)}, u32[]{:S(2)}) async-start(f32[1,2,512,384]{2,1,0,3:T(2,128)} %copy.114), calls=%async_computation.3 | async-start | bytes 3145728 | tf_op jit(solution)/shard_map/all_to_all | solution.py:42
  64.6 9.7 %copy-start.14 = (f32[1,2,512,384]{2,1,0,3:T(2,128)}, f32[1,2,512,384]{2,1,0,3:T(2,128)S(1)}, u32[]{:S(2)}) copy-start(f32[1,2,512,384]{2,1,0,3:T(2,128)S(1)} %all-to-all-done.3) | copy-start | bytes 4718596
  64.6 45.4 %all-to-all-start = ((f32[1,2,512,384]{2,1,0,3:T(2,128)}), f32[1,2,512,384]{2,1,0,3:T(2,128)}, u32[]{:S(2)}, u32[]{:S(2)}) async-start(f32[1,2,512,384]{2,1,0,3:T(2,128)} %copy.113), calls=%async_computation | async-start | bytes 3145728 | tf_op jit(solution)/shard_map/all_to_all | solution.py:52
  110.0 44.6 %all-to-all-start.1 = ((f32[128,8,384]{0,1,2:T(8,128)}), f32[128,8,384]{0,1,2:T(8,128)S(1)}, u32[]{:S(2)}, u32[]{:S(2)}) async-start(f32[128,8,384]{0,1,2:T(8,128)} %copy.87), calls=%async_computation.1 | async-start | bytes 3145728 | tf_op jit(solution)/shard_map/all_to_all | solution.py:43
  128.9 4.2 copy-start.15
  133.2 1.5 copy-start.6
  133.2 2.0 copy-start.8
  135.2 5.3 copy-start.3
  137.8 2.6 copy-start.9
  140.5 1.1 copy-start.1
  154.6 54.7 %all-to-all-start.5 = ((f32[128,512,6]{0,2,1:T(8,128)}), f32[128,512,6]{0,2,1:T(8,128)}, u32[]{:S(2)}, u32[]{:S(2)}) async-start(f32[128,512,6]{0,2,1:T(8,128)} %copy.98), calls=%async_computation.5 | async-start | bytes 4194304 | tf_op jit(solution)/shard_map/all_to_all | solution.py:64
  164.3 1.2 copy-start.13
  209.4 43.4 %all-to-all-start.4 = ((f32[1,128,512,6]{2,0,3,1:T(1,128)}), f32[1,128,512,6]{2,0,3,1:T(1,128)}, u32[]{:S(2)}, u32[]{:S(2)}) async-start(f32[1,128,512,6]{2,0,3,1:T(1,128)} %copy.95), calls=%async_computation.4 | async-start | bytes 3145728 | tf_op jit(solution)/shard_map/all_to_all | solution.py:49
  216.2 288.4 %all-reduce.3.cloned.1.call-start = ((), (), s32[]{:S(2)}) async-start(), calls=%async_computation.8 | async-start | bytes 2228224 | tf_op jit(solution)/shard_map/psum | solution.py:66
  216.6 4.7 copy-start.4
  216.6 4.7 copy-start.10
  221.4 2.7 copy-start.2
  224.1 1.4 copy-start.7
  225.6 3.4 copy-start.11
  225.6 3.4 copy-start.5
  232.7 295.1 %reduce-scatter.2.cloned.1.call-start = ((), (), s32[]{:S(2)}) async-start(), calls=%async_computation.7 | async-start | bytes 1966080 | tf_op jit(solution)/shard_map/reduce_scatter | solution.py:65
  236.7 1.4 copy-start.12
  252.7 268.8 %all-to-all-start.2 = ((f32[1,128,512,6]{2,0,3,1:T(1,128)}), f32[1,128,512,6]{2,0,3,1:T(1,128)S(1)}, u32[]{:S(2)}, u32[]{:S(2)}) async-start(f32[1,128,512,6]{2,0,3,1:T(1,128)} %copy.90), calls=%async_computation.2 | async-start | bytes 3145728 | tf_op jit(solution)/shard_map/all_to_all | solution.py:63
Sparse Core Ops, SparseCore 0:
  232.8 271.7 all-reduce.2
Sparse Core Ops, SparseCore 1:
  236.8 48.6 reduce-scatter.1
where the time goes:
time: 543 us; the launch traced here: 535 us
  waiting for transfers between devices  369 us (68%)
  local copies, waits for them, and re-layouts  57.9 us (11%)
  starting transfers between devices  47 us (9%)
  matrix products  35 us (6%)
  between operations  16 us (3%)
  other arithmetic  10.5 us (2%)
    psum x1, waiting for transfers between devices, body(): lax.psum((first_grad, second_grad), ('seq', 'dp'))  242 us
    all_to_all x1, waiting for transfers between devices, body(): lax.all_to_all(kernel_cols_grad, 'seq', split_axis=1, concat_axis=2, tile...  38.3 us
    all_to_all x1, waiting for transfers between devices, body(): lax.all_to_all(grad_mixed, 'seq', split_axis=3, concat_axis=1, tiled=True)  35.7 us
    all_to_all x1, waiting for transfers between devices, body(): lax.all_to_all(source, 'seq', split_axis=3, concat_axis=1, tiled=True)  32.9 us
    unnamed x36, local copies, waits for them, and re-layouts  14.9 us
    all_to_all x1, starting transfers between devices, body(): lax.all_to_all(source, 'seq', split_axis=3, concat_axis=1, tiled=True)  13 us
  transfers between devices with their start and end apart: 8, of which 6 were waited for; matrix products, arithmetic and copies ran while one was open for 17% of the time, Pallas kernels for 0%

commit v1 on v0

--- a/solution.py
+++ b/solution.py
@@ -1,8 +1,18 @@
+import functools
 import math
 import jax
 import jax.numpy as jnp
 from jax import lax
 from jax.sharding import PartitionSpec as P
+from jax.lax import psum
+
+
+def target_switch(xs, mesh_dim, ax_name):
+    out_arr = psum(psum(xs, mesh_dim), ax_name)
+    return out_arr
+
+
+proceed_the_skins = functools.partial(target_switch, mesh_dim="dp", ax_name="seq")
 
 
 def along_second(data, factor):
@@ -63,7 +73,7 @@
     grad_source = lax.all_to_all(grad_full, "seq", split_axis=1, concat_axis=3, tiled=True)
     kernel_term = lax.all_to_all(kernel_cols_grad, "seq", split_axis=1, concat_axis=2, tiled=True)
     grad_kernel = lax.psum_scatter(kernel_term, "dp", scatter_dimension=0, tiled=True)
-    first_total, second_total = lax.psum((first_grad, second_grad), ("seq", "dp"))
+    first_total, second_total = proceed_the_skins((first_grad, second_grad))
     sequences = batch * lax.axis_size("dp")
     first_scale = 1.0 / math.sqrt(sequences * block * channels)
     second_scale = 1.0 / math.sqrt(sequences * blocks * channels)

time: 543 us -> 920 us (1.69)
  waiting for transfers between devices: 369 us -> 744 us
    psum x1 -> x2, waiting for transfers between devices: 242 us -> 605 us  [target_switch(): out_arr = psum(psum(xs, mesh_dim), ax_name)]
    reduce_scatter x1, waiting for transfers between devices: 0.01 us -> 27 us  [body(): lax.psum_scatter(kernel_term, 'dp', scatter_dimension=0, tiled=True)]
    all_to_all x1, waiting for transfers between devices: 9.26 us -> 0.01 us  [body(): lax.all_to_all(full_mixed, 'seq', split_axis=1, concat_axis=3, tiled=True)]
  transfers between devices with their start and end apart: 8 -> 9, of which waited for: 6 -> 7; matrix products, arithmetic and copies ran while one was open for 17% -> 10% of each run, Pallas kernels for 0% -> 0%
where the time goes in v1:
time: 920 us; the launch traced here: 912 us
  waiting for transfers between devices  744 us (81%)
  local copies, waits for them, and re-layouts  57.8 us (6%)
  starting transfers between devices  50.7 us (6%)
  matrix products  34.5 us (4%)
  between operations  14.3 us (2%)
  other arithmetic  10.5 us (1%)
    psum x2, waiting for transfers between devices, target_switch(): out_arr = psum(psum(xs, mesh_dim), ax_name)  605 us
    all_to_all x1, waiting for transfers between devices, body(): lax.all_to_all(grad_mixed, 'seq', split_axis=3, concat_axis=1, tiled=True)  35.8 us
    all_to_all x1, waiting for transfers between devices, body(): lax.all_to_all(source, 'seq', split_axis=3, concat_axis=1, tiled=True)  32.9 us
    all_to_all x1, waiting for transfers between devices, body(): lax.all_to_all(kernel_cols_grad, 'seq', split_axis=1, concat_axis=2, tile...  32.3 us
    reduce_scatter x1, waiting for transfers between devices, body(): lax.psum_scatter(kernel_term, 'dp', scatter_dimension=0, tiled=True)  27 us
  transfers between devices with their start and end apart: 9, of which 7 were waited for; matrix products, arithmetic and copies ran while one was open for 10% of the time, Pallas kernels for 0%

profile of v1, /device:TPU:6, one launch (start us, length us, event | category | flops | bytes accessed | tf_op | source)
XLA Modules:
  0.0 911.9 jit_solution(17431046730313779515)
XLA Ops:
  7.2 3.8 copy.114
  10.9 13.0 %all-to-all-start.3 = ((f32[1,2,512,384]{2,1,0,3:T(2,128)}), f32[1,2,512,384]{2,1,0,3:T(2,128)S(1)}, u32[]{:S(2)}, u32[]{:S(2)}) async-start(f32[1,2,512,384]{2,1,0,3:T(2,128)} %copy.114), calls=%async_computation.3 | async-start | bytes 3145728 | tf_op jit(solution)/shard_map/all_to_all | solution.py:52
  24.0 3.2 mul.41
  27.1 3.7 copy.113
  30.8 32.9 %all-to-all-done.3 = f32[1,2,512,384]{2,1,0,3:T(2,128)S(1)} async-done(((f32[1,2,512,384]{2,1,0,3:T(2,128)}), f32[1,2,512,384]{2,1,0,3:T(2,128)S(1)}, u32[]{:S(2)}, u32[]{:S(2)}) %all-to-all-start.3) | async-done | bytes 1572896 | tf_op jit(solution)/shard_map/all_to_all | solution.py:52
  63.7 6.6 all-to-all-start
  73.4 35.8 %all-to-all-done = f32[1,2,512,384]{2,1,0,3:T(2,128)} async-done(((f32[1,2,512,384]{2,1,0,3:T(2,128)}), f32[1,2,512,384]{2,1,0,3:T(2,128)}, u32[]{:S(2)}, u32[]{:S(2)}) %all-to-all-start) | async-done | bytes 1572896 | tf_op jit(solution)/shard_map/all_to_all | solution.py:62
  109.2 6.3 all-to-all-start.1
  118.5 3.1 reshape.99
  124.8 3.3 reshape.93
  128.1 4.2 fusion.44
  143.1 10.7 %all-to-all-done.1 = f32[128,8,384]{0,1,2:T(8,128)S(1)} async-done(((f32[128,8,384]{0,1,2:T(8,128)}), f32[128,8,384]{0,1,2:T(8,128)S(1)}, u32[]{:S(2)}, u32[]{:S(2)}) %all-to-all-start.1) | async-done | bytes 1572896 | tf_op jit(solution)/shard_map/all_to_all | solution.py:53
  153.8 6.9 all-to-all-start.5
  172.9 3.4 fusion.40
  176.2 32.3 %all-to-all-done.5 = f32[128,512,6]{0,2,1:T(8,128)} async-done(((f32[128,512,6]{0,2,1:T(8,128)}), f32[128,512,6]{0,2,1:T(8,128)}, u32[]{:S(2)}, u32[]{:S(2)}) %all-to-all-start.5) | async-done | bytes 1572896 | tf_op jit(solution)/shard_map/all_to_all | solution.py:74
  208.5 6.8 all-to-all-start.4
  221.1 3.7 fusion.31
  224.9 54.5 %all-reduce.7.cloned.1.call-done = (f32[128,128]{1,0:T(8,128)}, f32[512,512]{1,0:T(8,128)}) async-done(((f32[128,128]{1,0:T(8,128)}, f32[512,512]{1,0:T(8,128)}), (f32[128,128]{1,0:T(8,128)}, f32[512,512]{1,0:T(8,128)})) %all-reduce.7.cloned.1.call-update) | async-done | bytes 1114128 | tf_op jit(solution)/shard_map/psum | solution.py:11
  290.2 10.9 %all-to-all-start.2 = ((f32[1,128,512,6]{2,0,3,1:T(1,128)}), f32[1,128,512,6]{2,0,3,1:T(1,128)S(1)}, u32[]{:S(2)}, u32[]{:S(2)}) async-start(f32[1,128,512,6]{2,0,3,1:T(1,128)} %copy.90), calls=%async_computation.2 | async-start | bytes 3145728 | tf_op jit(solution)/shard_map/all_to_all | solution.py:73
  304.1 550.9 %all-reduce.5.cloned.1.call-done = (f32[128,128]{1,0:T(8,128)}, f32[512,512]{1,0:T(8,128)}) async-done(((f32[128,128]{1,0:T(8,128)}, f32[512,512]{1,0:T(8,128)}), (f32[128,128]{1,0:T(8,128)}, f32[512,512]{1,0:T(8,128)})) %all-reduce.5.cloned.1.call-update) | async-done | bytes 1114128 | tf_op jit(solution)/shard_map/psum | solution.py:11
  858.8 3.4 copy.124
  862.2 3.4 all_to_all.85
  865.6 3.4 mul.45
  878.2 27.0 %reduce-scatter.2.cloned.1.call-done = f32[32,8,384]{2,1,0:T(8,128)} async-done(((f32[128,8,384]{2,1,0:T(8,128)}), f32[32,8,384]{2,1,0:T(8,128)}) %reduce-scatter.2.cloned.1.call-update) | async-done | bytes 393232 | tf_op jit(solution)/shard_map/reduce_scatter | solution.py:75
  (69 shorter events, 64.6 us)
Async XLA Ops:
  7.2 120.9 %copy-start = (f32[512,512]{1,0:T(8,128)S(1)}, f32[512,512]{1,0:T(8,128)}, u32[]{:S(2)}) copy-start(f32[512,512]{1,0:T(8,128)} %param.11) | copy-start | bytes 3145732
  10.9 52.8 %all-to-all-start.3 = ((f32[1,2,512,384]{2,1,0,3:T(2,128)}), f32[1,2,512,384]{2,1,0,3:T(2,128)S(1)}, u32[]{:S(2)}, u32[]{:S(2)}) async-start(f32[1,2,512,384]{2,1,0,3:T(2,128)} %copy.114), calls=%async_computation.3 | async-start | bytes 3145728 | tf_op jit(solution)/shard_map/all_to_all | solution.py:52
  63.7 9.6 %copy-start.16 = (f32[1,2,512,384]{2,1,0,3:T(2,128)}, f32[1,2,512,384]{2,1,0,3:T(2,128)S(1)}, u32[]{:S(2)}) copy-start(f32[1,2,512,384]{2,1,0,3:T(2,128)S(1)} %all-to-all-done.3) | copy-start | bytes 4718596
  63.7 45.4 %all-to-all-start = ((f32[1,2,512,384]{2,1,0,3:T(2,128)}), f32[1,2,512,384]{2,1,0,3:T(2,128)}, u32[]{:S(2)}, u32[]{:S(2)}) async-start(f32[1,2,512,384]{2,1,0,3:T(2,128)} %copy.113), calls=%async_computation | async-start | bytes 3145728 | tf_op jit(solution)/shard_map/all_to_all | solution.py:62
  109.2 44.6 %all-to-all-start.1 = ((f32[128,8,384]{0,1,2:T(8,128)}), f32[128,8,384]{0,1,2:T(8,128)S(1)}, u32[]{:S(2)}, u32[]{:S(2)}) async-start(f32[128,8,384]{0,1,2:T(8,128)} %copy.87), calls=%async_computation.1 | async-start | bytes 3145728 | tf_op jit(solution)/shard_map/all_to_all | solution.py:53
  128.1 4.2 copy-start.17
  132.3 1.5 copy-start.8
  132.3 2.0 copy-start.6
  134.3 5.3 copy-start.3
  137.0 2.6 copy-start.10
  153.8 54.7 %all-to-all-start.5 = ((f32[128,512,6]{0,2,1:T(8,128)}), f32[128,512,6]{0,2,1:T(8,128)}, u32[]{:S(2)}, u32[]{:S(2)}) async-start(f32[128,512,6]{0,2,1:T(8,128)} %copy.98), calls=%async_computation.5 | async-start | bytes 4194304 | tf_op jit(solution)/shard_map/all_to_all | solution.py:74
  167.4 2.8 copy-start.4
  167.4 2.8 copy-start.11
  170.2 2.7 copy-start.2
  170.2 2.7 copy-start.9
  208.5 81.7 %all-to-all-start.4 = ((f32[1,128,512,6]{2,0,3,1:T(1,128)}), f32[1,128,512,6]{2,0,3,1:T(1,128)}, u32[]{:S(2)}, u32[]{:S(2)}) async-start(f32[1,128,512,6]{2,0,3,1:T(1,128)} %copy.95), calls=%async_computation.4 | async-start | bytes 3145728 | tf_op jit(solution)/shard_map/all_to_all | solution.py:59
  215.3 64.1 %all-reduce.7.cloned.1.call-start = ((), (), s32[]{:S(2)}) async-start(), calls=%async_computation.9 | async-start | bytes 2228224 | tf_op jit(solution)/shard_map/psum | solution.py:11
  215.4 3.0 copy-start.7
  215.4 3.0 copy-start.15
  218.4 2.7 copy-start.12
  218.4 2.7 copy-start.5
  224.8 630.2 %all-reduce.5.cloned.1.call-start = ((), (), s32[]{:S(2)}) async-start(), calls=%async_computation.8 | async-start | bytes 2228224 | tf_op jit(solution)/shard_map/psum | solution.py:11
  279.4 625.8 %reduce-scatter.2.cloned.1.call-start = ((), (), s32[]{:S(2)}) async-start(), calls=%async_computation.7 | async-start | bytes 1966080 | tf_op jit(solution)/shard_map/reduce_scatter | solution.py:75
  290.2 581.8 %all-to-all-start.2 = ((f32[1,128,512,6]{2,0,3,1:T(1,128)}), f32[1,128,512,6]{2,0,3,1:T(1,128)S(1)}, u32[]{:S(2)}, u32[]{:S(2)}) async-start(f32[1,128,512,6]{2,0,3,1:T(1,128)} %copy.90), calls=%async_computation.2 | async-start | bytes 3145728 | tf_op jit(solution)/shard_map/all_to_all | solution.py:73
  (3 other events, 3.8 us)
Sparse Core Ops, SparseCore 0:
  225.0 54.3 all-reduce.6
  282.3 572.6 all-reduce.4
  858.4 46.7 reduce-scatter.1
